TPU v7x, 32 devices: a whole 2x2x4 slice. The times are simulated.
32 devices in a mesh: groups: 2 (over x), rows: 16 (over z, y, core).
Axes of the slice: x: 2, y: 2, z: 4, core: 2. Of those that a mesh axis runs over, the one named last changes fastest.
Arguments:
- response: float32 [1536, 128, 128], P(('groups', 'rows')), parts along dimension 0, may hold values from 0.0001 to 0.01
- block_row: int32 [1536], P(('groups', 'rows')), parts along dimension 0, may hold values from 0 to 7, as said below
- block_col: int32 [1536], P(('groups', 'rows')), parts along dimension 0, may hold values from 0 to 207, as said below
- counts: int32 [64, 32768], P(None, ('groups', 'rows')), parts along dimension 1, may hold values from 1 to 16
- prior: float32 [53248], P(('groups', 'rows')), parts along dimension 0, may hold values from 0.5 to 5
Outputs:
- unfolded: float32 [64, 53248], P(None, ('groups', 'rows')), parts along dimension 1
There are 2 independent parts, one for each index of `groups`. A program takes and returns all parts, laid end to end along the dimension named above; each array names one. Nothing has to cross between parts.
Inputs may be any that keep to these rules, and one draw needn't show every extreme that they name: `block_col`: each device's 48 blocks come in 16 groups of 3; group o holds block columns o * 13 to (o + 1) * 13 - 1, distinct within the group; every block column holds at least one block. `block_row`: every block row of every device holds at least one block.
All inputs are finite; a program needn't handle non-finite values.
Results may differ from a plain program's by a relative error of at most 0.0001.
Values sent between devices are 32-bit elements; how exact they have to be, the bound alone decides.
A program may use at most 128 MiB of HBM per device.

v0:
```python
import jax
import jax.numpy as jnp
from jax import lax
from jax.sharding import PartitionSpec as P


def fold_full(response, estimate, wanted, peer_count, per_owner):
    slot_count = response.shape[0]
    replicas = estimate.shape[1]
    block_size = estimate.shape[2]
    picked = jnp.take(estimate, wanted, axis=0)
    arrived = lax.all_to_all(
        picked.reshape(peer_count, per_owner, replicas, block_size),
        "rows",
        split_axis=0,
        concat_axis=0,
        tiled=True,
    )
    return jnp.einsum(
        "sic,src->sri",
        response,
        arrived.reshape(slot_count, replicas, block_size),
        precision=lax.Precision.HIGHEST,
    )


def send_back(backward):
    return lax.all_to_all(backward, "rows", split_axis=0, concat_axis=0, tiled=True)


def local(response, block_row, block_col, counts, prior):
    highest = lax.Precision.HIGHEST
    peer_count = lax.axis_size("rows")
    slot_count = response.shape[0]
    per_owner = slot_count // peer_count
    block_size = response.shape[1]
    replicas = counts.shape[0]
    row_blocks = counts.shape[1] // block_size
    col_blocks = prior.shape[0] // block_size
    local_column = block_col % col_blocks
    wanted = lax.all_to_all(
        local_column.reshape(peer_count, per_owner), "rows", split_axis=0, concat_axis=0, tiled=True
    ).reshape(slot_count)
    owner_pick = (wanted[:, None] == jnp.arange(col_blocks, dtype=jnp.int32)[None, :]).astype(
        jnp.float32
    )
    row_pick = (block_row[:, None] == jnp.arange(row_blocks, dtype=jnp.int32)[None, :]).astype(
        jnp.float32
    )
    column_mass = jnp.sum(response, axis=1)
    mass_shaped = column_mass.reshape(peer_count, per_owner, block_size)
    efficiency = None
    mass_back = lax.all_to_all(mass_shaped, "rows", split_axis=0, concat_axis=0, tiled=True)
    efficiency = jnp.einsum(
        "sk,sb->kb", owner_pick, mass_back.reshape(slot_count, block_size), precision=highest
    )
    prior_blocks = prior.reshape(col_blocks, block_size)
    estimate = jnp.broadcast_to(prior_blocks[:, None, :], (col_blocks, replicas, block_size))
    measured = (
        counts.reshape(replicas, row_blocks, block_size).transpose(1, 0, 2).astype(jnp.float32)
    )
    contrib = fold_full(response, estimate, wanted, peer_count, per_owner)
    folded = jnp.einsum("sb,sri->bri", row_pick, contrib, precision=highest)
    ratios = measured / folded
    spread = jnp.take(ratios, block_row, axis=0)
    backward = jnp.einsum("sic,sri->src", response, spread, precision=highest)
    backward = backward.reshape(peer_count, per_owner, replicas, block_size)
    returned = send_back(backward)
    gathered = jnp.einsum(
        "sk,srb->krb",
        owner_pick,
        returned.reshape(slot_count, replicas, block_size),
        precision=highest,
    )
    estimate = estimate * gathered / efficiency[:, None, :]
    contrib = fold_full(response, estimate, wanted, peer_count, per_owner)
    folded = jnp.einsum("sb,sri->bri", row_pick, contrib, precision=highest)
    ratios = measured / folded
    spread = jnp.take(ratios, block_row, axis=0)
    backward = jnp.einsum("sic,sri->src", response, spread, precision=highest)
    returned = send_back(backward.reshape(peer_count, per_owner, replicas, block_size))
    gathered = jnp.einsum(
        "sk,srb->krb",
        owner_pick,
        returned.reshape(slot_count, replicas, block_size),
        precision=highest,
    )
    estimate = estimate * gathered / efficiency[:, None, :]
    return estimate.transpose(1, 0, 2).reshape(replicas, col_blocks * block_size)


def solution(mesh):
    in_specs = (
        P(("groups", "rows"), None, None),
        P(("groups", "rows")),
        P(("groups", "rows")),
        P(None, ("groups", "rows")),
        P(("groups", "rows")),
    )
    out_specs = P(None, ("groups", "rows"))
    return jax.shard_map(local, mesh=mesh, in_specs=in_specs, out_specs=out_specs, check_vma=False)
```

profile of v0, /device:TPU:1, one launch (start us, length us, event | category | flops | bytes accessed | tf_op | source)
XLA Modules:
  0.0 230.6 jit_solution(528757432289032884)
XLA Ops:
  0.0 0.7 and_select_fusion
  0.7 0.1 all_to_all.21
  0.7 12.9 %all_to_all.34 = s32[16,1,3]{2,1,0:T(1,128)S(1)} all-to-all(s32[16,1,3]{2,1,0:T(1,128)S(1)} %bitcast.45), channel_id=1, replica_groups=mesh['groups'=2,'rows'=16] {'rows'}, dimensions={0} | all-to-all | bytes 384 | tf_op jit(solution)/shard_map/all_to_all | solution.py:41
  13.7 0.5 broadcast.30
  14.2 0.7 reduce.3
  14.9 0.1 eq.30
  15.0 0.7 broadcast_in_dim.31.clone
  15.7 0.6 gather_fusion
  16.4 1.3 broadcast_select_fusion.1
  17.7 5.1 %all-to-all-start.1 = ((f32[16,3,64,128]{3,2,1,0:T(8,128)}), f32[16,3,64,128]{3,2,1,0:T(8,128)}, u32[]{:S(2)}, u32[]{:S(2)}) async-start(f32[16,3,64,128]{3,2,1,0:T(8,128)} %bitcast.37), calls=%async_computation.1 | async-start | bytes 3145728 | tf_op jit(solution)/shard_map/all_to_all | solution.py:12
  22.8 0.0 copy-done
  22.8 0.0 copy-start.5
  22.8 0.0 copy-start.7
  22.9 0.3 reduce_sum.9
  23.2 0.6 reshape.60
  23.8 0.0 copy-done.5
  23.9 0.0 copy-done.7
  23.9 0.0 copy-start.1
  23.9 31.4 %all-to-all-done.1 = f32[16,3,64,128]{3,2,1,0:T(8,128)} async-done(((f32[16,3,64,128]{3,2,1,0:T(8,128)}), f32[16,3,64,128]{3,2,1,0:T(8,128)}, u32[]{:S(2)}, u32[]{:S(2)}) %all-to-all-start.1) | async-done | bytes 1572896 | tf_op jit(solution)/shard_map/all_to_all | solution.py:12
  55.3 8.7 %all-to-all-start.3 = ((f32[16,3,128]{2,1,0:T(4,128)}), f32[16,3,128]{2,1,0:T(4,128)S(1)}, u32[]{:S(2)}, u32[]{:S(2)}) async-start(f32[16,3,128]{2,1,0:T(4,128)} %reshape.60), calls=%async_computation.3 | async-start | bytes 65536 | tf_op jit(solution)/shard_map/all_to_all | solution.py:53
  64.0 7.6 %fusion.48 = f32[48,64,128]{2,1,0:T(8,128)S(1)} fusion(f32[48,64,128]{2,1,0:T(8,128)} %bitcast.6, f32[48,128,128]{2,1,0:T(8,128)S(1)} %copy-done), kind=kOutput, calls=%fused_computation.49 | convolution fusion | flops 603979776 | bytes 6291456 | tf_op jit(solution)/shard_map/sic,src->sri/dot_general | solution.py:19
  71.7 0.0 copy-done.1
  71.7 1.5 fusion.24
  73.2 0.1 copy.23
  73.3 1.8 gather_fusion.1
  75.1 5.5 %fusion.10 = f32[48,64,128]{2,1,0:T(8,128)} fusion(f32[48,128,128]{2,1,0:T(8,128)S(1)} %copy-done, f32[48,64,128]{2,1,0:T(8,128)} %gather_fusion.1, pred[48]{0:T(512)(128)(4,1)S(1)} %compare_and_fusion), kind=kOutput, calls=%fused_computation.14 | convolution fusion | flops 604372992 | bytes 6291504 | tf_op jit(solution)/shard_map/sic,sri->src/dot_general | solution.py:66
  80.6 0.0 all-to-all-done.3
  80.6 6.2 %all-to-all-start.2 = ((f32[16,3,64,128]{3,2,1,0:T(8,128)}), f32[16,3,64,128]{3,2,1,0:T(8,128)}, u32[]{:S(2)}, u32[]{:S(2)}) async-start(f32[16,3,64,128]{3,2,1,0:T(8,128)} %bitcast.38), calls=%async_computation.2 | async-start | bytes 3145728 | tf_op jit(solution)/shard_map/all_to_all | solution.py:28
  86.8 0.1 fusion.34
  86.9 32.3 %all-to-all-done.2 = f32[16,3,64,128]{3,2,1,0:T(8,128)} async-done(((f32[16,3,64,128]{3,2,1,0:T(8,128)}), f32[16,3,64,128]{3,2,1,0:T(8,128)}, u32[]{:S(2)}, u32[]{:S(2)}) %all-to-all-start.2) | async-done | bytes 1572896 | tf_op jit(solution)/shard_map/all_to_all | solution.py:28
  119.2 0.0 copy-done.6
  119.2 2.8 %fusion.15 = f32[13,64,128]{2,0,1:T(8,128)S(1)} fusion(f32[48,64,128]{2,1,0:T(8,128)} %bitcast.8, f32[13,128]{1,0:T(8,128)S(1)} %fusion.34, f32[13,128]{1,0:T(8,128)S(1)} %bitcast.47, s32[48]{0:T(128)S(1)} %eq.30), kind=kOutput, calls=%fused_computation.17 | convolution fusion | flops 61555312 | bytes 2012352 | tf_op jit(solution)/shard_map/sk,srb->krb/dot_general | solution.py:69
  122.0 0.0 copy-start.3
  122.0 0.8 copy-done.3
  122.8 0.9 copy.25
  123.7 2.8 %gather_fusion.2 = f32[48,64,128]{2,1,0:T(8,128)} fusion(f32[13,64,128]{2,1,0:T(8,128)} %copy.25, s32[1024]{0:T(1024)S(1)} %pad_clamp_fusion.1), kind=kCustom, calls=%fused_computation.2.clone | custom fusion | bytes 3145920 | tf_op jit(solution)/shard_map/jit(_take)/gather | solution.py:11
  126.5 1.6 broadcast_select_fusion
  128.1 45.0 %all_to_all.35 = f32[16,3,64,128]{3,2,1,0:T(8,128)S(1)} all-to-all(f32[16,3,64,128]{3,2,1,0:T(8,128)S(1)} %bitcast.39), channel_id=1, replica_groups=mesh['groups'=2,'rows'=16] {'rows'}, dimensions={0} | all-to-all | bytes 3145728 | tf_op jit(solution)/shard_map/all_to_all | solution.py:12
  173.1 6.2 %fusion.49 = f32[48,64,128]{2,1,0:T(8,128)S(1)} fusion(f32[48,64,128]{2,1,0:T(8,128)S(1)} %bitcast.41, f32[48,128,128]{2,1,0:T(8,128)S(1)} %copy-done), kind=kOutput, calls=%fused_computation.50 | convolution fusion | flops 603979776 | bytes 6291456 | tf_op jit(solution)/shard_map/sic,src->sri/dot_general | solution.py:19
  179.3 0.0 copy-done.2
  179.3 1.5 fusion.27
  180.8 0.1 copy.27
  180.9 1.8 gather_fusion.3
  182.7 4.4 %fusion.8 = f32[48,64,128]{2,1,0:T(8,128)S(1)} fusion(f32[48,128,128]{2,1,0:T(8,128)S(1)} %copy-done, f32[48,64,128]{2,1,0:T(8,128)} %gather_fusion.3, pred[48]{0:T(512)(128)(4,1)S(1)} %compare_and_fusion), kind=kOutput, calls=%fused_computation.12 | convolution fusion | flops 604372992 | bytes 6291504 | tf_op jit(solution)/shard_map/sic,sri->src/dot_general | solution.py:80
  187.1 41.0 %all_to_all.36 = f32[16,3,64,128]{3,2,1,0:T(8,128)S(1)} all-to-all(f32[16,3,64,128]{3,2,1,0:T(8,128)S(1)} %bitcast.40), channel_id=1, replica_groups=mesh['groups'=2,'rows'=16] {'rows'}, dimensions={0} | all-to-all | bytes 3145728 | tf_op jit(solution)/shard_map/all_to_all | solution.py:28
  228.2 0.0 copy-done.4
  228.2 1.5 fusion.21
  229.7 0.9 copy.53
  (13 shorter events, 0.1 us)
Async XLA Ops:
  17.7 5.1 %copy-start = (f32[48,128,128]{2,1,0:T(8,128)S(1)}, f32[48,128,128]{2,1,0:T(8,128)}, u32[]{:S(2)}) copy-start(f32[48,128,128]{2,1,0:T(8,128)} %param.9) | copy-start | bytes 9437188
  17.7 37.6 %all-to-all-start.1 = ((f32[16,3,64,128]{3,2,1,0:T(8,128)}), f32[16,3,64,128]{3,2,1,0:T(8,128)}, u32[]{:S(2)}, u32[]{:S(2)}) async-start(f32[16,3,64,128]{3,2,1,0:T(8,128)} %bitcast.37), calls=%async_computation.1 | async-start | bytes 3145728 | tf_op jit(solution)/shard_map/all_to_all | solution.py:12
  22.8 1.0 copy-start.5
  22.8 1.0 copy-start.7
  23.9 47.8 %copy-start.1 = (f32[8,8,8,128]{3,2,1,0:T(8,128)}, f32[8,8,8,128]{3,2,1,0:T(8,128)S(1)}, u32[]{:S(2)}) copy-start(f32[8,8,8,128]{3,2,1,0:T(8,128)S(1)} %copy.30) | copy-start | bytes 786436
  55.3 25.3 %all-to-all-start.3 = ((f32[16,3,128]{2,1,0:T(4,128)}), f32[16,3,128]{2,1,0:T(4,128)S(1)}, u32[]{:S(2)}, u32[]{:S(2)}) async-start(f32[16,3,128]{2,1,0:T(4,128)} %reshape.60), calls=%async_computation.3 | async-start | bytes 65536 | tf_op jit(solution)/shard_map/all_to_all | solution.py:53
  80.6 38.6 %copy-start.6 = (f32[1664]{0:T(1024)S(1)}, f32[1664]{0:T(1024)}, u32[]{:S(2)}) copy-start(f32[1664]{0:T(1024)} %param.13) | copy-start | bytes 19972
  80.6 38.6 %all-to-all-start.2 = ((f32[16,3,64,128]{3,2,1,0:T(8,128)}), f32[16,3,64,128]{3,2,1,0:T(8,128)}, u32[]{:S(2)}, u32[]{:S(2)}) async-start(f32[16,3,64,128]{3,2,1,0:T(8,128)} %bitcast.38), calls=%async_computation.2 | async-start | bytes 3145728 | tf_op jit(solution)/shard_map/all_to_all | solution.py:28
  122.0 0.8 copy-start.3
  173.1 6.2 %copy-start.2 = (f32[8,8,8,128]{3,2,1,0:T(8,128)S(1)}, f32[8,8,8,128]{3,2,1,0:T(8,128)}, u32[]{:S(2)}) copy-start(f32[8,8,8,128]{3,2,1,0:T(8,128)} %copy-done.1) | copy-start | bytes 786436
  187.1 41.1 %copy-start.4 = (f32[13,64,128]{2,0,1:T(8,128)S(1)}, f32[13,64,128]{2,0,1:T(8,128)}, u32[]{:S(2)}) copy-start(f32[13,64,128]{2,0,1:T(8,128)} %copy-done.3) | copy-start | bytes 1277956
where the time goes:
time: 231 us
  blocking collectives  99 us (43%)
  waiting for transfers between devices  63.7 us (28%)
  matrix products  31.2 us (14%)
  starting transfers between devices  20 us (9%)
  local copies, waits for them, and re-layouts  11.8 us (5%)
  other arithmetic  4.59 us (2%)
    all_to_all x1, blocking collectives, fold_full(): lax.all_to_all(picked.reshape(peer_count, per_owner, replicas, block_size...  45 us
    all_to_all x1, blocking collectives, send_back(): lax.all_to_all(backward, 'rows', split_axis=0, concat_axis=0, tiled=True)  41 us
    all_to_all x1, waiting for transfers between devices, send_back(): lax.all_to_all(backward, 'rows', split_axis=0, concat_axis=0, tiled=True)  32.3 us
    all_to_all x1, waiting for transfers between devices, fold_full(): lax.all_to_all(picked.reshape(peer_count, per_owner, replicas, block_size...  31.4 us
    dot_general x2, matrix products, fold_full(): jnp.einsum('sic,src->sri', response, arrived.reshape(slot_count, replicas...  13.8 us
    all_to_all x1, blocking collectives, local(): lax.all_to_all(local_column.reshape(peer_count, per_owner), 'rows', split...  12.9 us
    dot_general x2, matrix products, local(): backward = jnp.einsum('sic,sri->src', response, spread, precision=highest)  9.94 us
    all_to_all x1, starting transfers between devices, local(): lax.all_to_all(mass_shaped, 'rows', split_axis=0, concat_axis=0, tiled=True)  8.73 us
  transfers between devices with their start and end apart: 3, of which 2 were waited for; matrix products, arithmetic and copies ran while one was open for 8% of the time, Pallas kernels for 0%

commit v1 on v0

v1 whole, which is shorter than its diff:
```python
import functools

import jax
import jax.numpy as jnp
from jax import lax
from jax.experimental import pallas as pl
from jax.experimental.pallas import tpu as pltpu
from jax.sharding import PartitionSpec as P

CHUNKS = 2
F32 = jnp.float32
BF16 = jnp.bfloat16


def split(x):
    high = x.astype(BF16).astype(F32)
    return jnp.concatenate([high, x - high], axis=0).astype(BF16)


def kernel(
    n, per, cols, rows, chunk_count,
    response, block_row, local_col, col_message, counts, prior,
    out,
    response_split, message, meta, wanted_landed, wanted, send, returned, fetched, estimate,
    ratio, inverse, send_sem, recv_sem, local_sem,
):
    blk = prior.shape[1]
    rc = counts.shape[0] // chunk_count
    me = lax.axis_index("rows")

    def peer_of(k):
        return lax.rem(me + k + 1, n)

    def remote(src, dst, index, peer):
        return pltpu.make_async_remote_copy(
            src_ref=src, dst_ref=dst, send_sem=send_sem.at[index], recv_sem=recv_sem.at[index],
            device_id={"rows": peer}, device_id_type=pl.DeviceIdType.MESH,
        )

    def wait_bytes(ref, sem):
        pltpu.make_async_copy(ref, ref, sem).wait()

    barrier = pltpu.get_barrier_semaphore()

    @pl.loop(0, n - 1)
    def _(k):
        pl.semaphore_signal(
            barrier, inc=1, device_id={"rows": peer_of(k)}, device_id_type=pl.DeviceIdType.MESH
        )

    @pl.loop(0, n)
    def _(p):
        message[p, 0:cols, :] = prior[...]
        for j in range(per):
            block = response[p * per + j]
            message[p, cols + j : cols + j + 1, :] = jnp.sum(block, axis=0, keepdims=True)
            response_split[p * per + j] = split(block)

    pl.semaphore_wait(barrier, n - 1)
    meta_index = 3 * chunk_count

    @pl.loop(0, n - 1)
    def _(k):
        peer = peer_of(k)
        remote(message.at[peer], meta.at[me], meta_index, peer).start()
        remote(col_message.at[peer], wanted_landed.at[me], meta_index + 1, peer).start()

    meta[me] = message[me]
    wanted_landed[me] = col_message[me]
    wait_bytes(meta.at[pl.ds(0, n - 1)], recv_sem.at[meta_index])

    def fold_prior(p, total):
        for j in range(per):
            s = p * per + j
            row = meta[p, pl.ds(local_col[s], 1), :]
            place = lax.broadcasted_iota(jnp.int32, (rows, blk), 0) == block_row[s]
            masked = jnp.where(place, jnp.broadcast_to(row, (rows, blk)), 0.0)
            total = total + lax.dot_general(
                split(masked), response_split[s], (((1,), (1,)), ((), ())), preferred_element_type=F32
            )
        return total

    total = lax.fori_loop(0, n, fold_prior, jnp.zeros((2 * rows, 2 * blk), F32))
    total = total[:rows] + total[rows:]
    first_fold = total[:, :blk] + total[:, blk:]

    def store_ratio(c, b, folded):
        measured = counts[c * rc : (c + 1) * rc, b * blk : (b + 1) * blk].astype(F32)
        ratio[b * chunk_count + c] = split(measured / folded)

    def backward(c, phase):
        def one(s):
            x = ratio[block_row[s] * chunk_count + c]
            both = jnp.dot(
                jnp.concatenate([x, x], axis=1), response_split[s], preferred_element_type=F32
            )
            return both[:rc] + both[rc:]

        @pl.loop(0, n - 1)
        def _(k):
            peer = peer_of(k)
            for j in range(per):
                send[c, peer * per + j] = one(peer * per + j)
            remote(
                send.at[c, pl.ds(peer * per, per)], returned.at[c, pl.ds(me * per, per)],
                phase * chunk_count + c, peer,
            ).start()

        for j in range(per):
            returned[c, me * per + j] = one(me * per + j)

    def wait_sent(c, phase):
        wait_bytes(send.at[c, pl.ds(0, (n - 1) * per)], send_sem.at[phase * chunk_count + c])

    def gather(c, phase):
        wait_bytes(returned.at[c, pl.ds(0, (n - 1) * per)], recv_sem.at[phase * chunk_count + c])

        def add(p, sums):
            sums = list(sums)
            for j in range(per):
                block = returned[c, p * per + j]
                w = wanted[p, 0, j]
                for k in range(cols):
                    sums[k] = sums[k] + block * (w == k).astype(F32)
            return tuple(sums)

        return lax.fori_loop(0, n, add, tuple(jnp.zeros((rc, blk), F32) for _ in range(cols)))

    def spread(c):
        @pl.loop(0, n - 1)
        def _(k):
            peer = peer_of(k)
            for j in range(per):
                send[c, peer * per + j] = estimate[c * cols + wanted[peer, 0, j]]
            remote(
                send.at[c, pl.ds(peer * per, per)], fetched.at[c, pl.ds(me * per, per)],
                chunk_count + c, peer,
            ).start()

        for j in range(per):
            fetched[c, me * per + j] = estimate[c * cols + wanted[me, 0, j]]

    def fold(c):
        wait_bytes(fetched.at[c, pl.ds(0, (n - 1) * per)], recv_sem.at[chunk_count + c])

        def add(p, sums):
            sums = list(sums)
            for j in range(per):
                s = p * per + j
                product = lax.dot_general(
                    split(fetched[c, s]), response_split[s], (((1,), (1,)), ((), ())),
                    preferred_element_type=F32,
                )
                product = product[:rc] + product[rc:]
                product = product[:, :blk] + product[:, blk:]
                r = block_row[s]
                for b in range(rows):
                    sums[b] = sums[b] + product * (r == b).astype(F32)
            return tuple(sums)

        sums = lax.fori_loop(0, n, add, tuple(jnp.zeros((rc, blk), F32) for _ in range(rows)))
        for b in range(rows):
            store_ratio(c, b, sums[b])

    for c in range(chunk_count):
        for b in range(rows):
            store_ratio(c, b, first_fold[b : b + 1])
        backward(c, 0)

    wait_bytes(wanted_landed.at[pl.ds(0, n - 1)], recv_sem.at[meta_index + 1])
    to_scalar = pltpu.make_async_copy(wanted_landed, wanted, local_sem)
    to_scalar.start()
    to_scalar.wait()

    def add_mass(p, sums):
        sums = list(sums)
        for j in range(per):
            mass = meta[p, cols + j : cols + j + 1, :]
            w = wanted[p, 0, j]
            for k in range(cols):
                sums[k] = sums[k] + mass * (w == k).astype(F32)
        return tuple(sums)

    masses = lax.fori_loop(0, n, add_mass, tuple(jnp.zeros((1, blk), F32) for _ in range(cols)))
    for k in range(cols):
        inverse[k : k + 1, :] = 1.0 / masses[k]

    for c in range(chunk_count):
        sums = gather(c, 0)
        for k in range(cols):
            estimate[c * cols + k] = (prior[k : k + 1, :] * inverse[k : k + 1, :]) * sums[k]
        wait_sent(c, 0)
        spread(c)
    for c in range(chunk_count):
        fold(c)
        wait_sent(c, 1)
        backward(c, 2)
    for c in range(chunk_count):
        sums = gather(c, 2)
        for k in range(cols):
            out[c * rc : (c + 1) * rc, k * blk : (k + 1) * blk] = (
                estimate[c * cols + k] * sums[k] * inverse[k : k + 1, :]
            )
        wait_sent(c, 2)
    wait_bytes(message.at[pl.ds(0, n - 1)], send_sem.at[meta_index])
    wait_bytes(wanted_landed.at[pl.ds(0, n - 1)], send_sem.at[meta_index + 1])


def local(response, block_row, block_col, counts, prior):
    n = lax.axis_size("rows")
    slots, blk, _ = response.shape
    per = slots // n
    reps = counts.shape[0]
    rows = counts.shape[1] // blk
    cols = prior.shape[0] // blk
    rc = reps // CHUNKS
    local_col = block_col % cols
    message_rows = -(-(cols + per) // 8) * 8
    col_message = jnp.pad(local_col.reshape(n, 1, per), ((0, 0), (0, 7), (0, blk - per)))
    vmem = pl.BlockSpec(memory_space=pltpu.VMEM)
    smem = pl.BlockSpec(memory_space=pltpu.SMEM)
    sems = 3 * CHUNKS + 2
    return pl.pallas_call(
        functools.partial(kernel, n, per, cols, rows, CHUNKS),
        out_shape=jax.ShapeDtypeStruct((reps, cols * blk), F32),
        in_specs=[vmem, smem, smem, vmem, vmem, vmem],
        out_specs=vmem,
        scratch_shapes=[
            pltpu.VMEM((slots, 2 * blk, blk), BF16),
            pltpu.VMEM((n, message_rows, blk), F32),
            pltpu.VMEM((n, message_rows, blk), F32),
            pltpu.VMEM((n, 8, blk), jnp.int32),
            pltpu.SMEM((n, 8, blk), jnp.int32),
            pltpu.VMEM((CHUNKS, slots, rc, blk), F32),
            pltpu.VMEM((CHUNKS, slots, rc, blk), F32),
            pltpu.VMEM((CHUNKS, slots, rc, blk), F32),
            pltpu.VMEM((CHUNKS * cols, rc, blk), F32),
            pltpu.VMEM((rows * CHUNKS, 2 * rc, blk), BF16),
            pltpu.VMEM((-(-cols // 8) * 8, blk), F32),
            pltpu.SemaphoreType.DMA((sems,)),
            pltpu.SemaphoreType.DMA((sems,)),
            pltpu.SemaphoreType.DMA,
        ],
        compiler_params=pltpu.CompilerParams(
            collective_id=0, has_side_effects=True, vmem_limit_bytes=60 * 1024 * 1024
        ),
    )(response, block_row, local_col, col_message, counts, prior.reshape(cols, blk))


def solution(mesh):
    in_specs = (
        P(("groups", "rows"), None, None),
        P(("groups", "rows")),
        P(("groups", "rows")),
        P(None, ("groups", "rows")),
        P(("groups", "rows")),
    )
    out_specs = P(None, ("groups", "rows"))
    return jax.shard_map(local, mesh=mesh, in_specs=in_specs, out_specs=out_specs, check_vma=False)
```

time: 231 us -> 125 us (0.54)
  the two profiles are of different devices: /device:TPU:1 before, /device:TPU:21 now
where the time goes in v1:
time: 125 us; the launch traced here: 124 us
  Pallas kernels  121 us (97%)
  local copies, waits for them, and re-layouts  2.52 us (2%)
    pallas_call x1, Pallas kernels, local(): pl.pallas_call(functools.partial(kernel, n, per, cols, rows, CHUNKS), out...  121 us

profile of v1, /device:TPU:21, one launch (start us, length us, event | category | flops | bytes accessed | tf_op | source)
XLA Modules:
  0.0 124.4 jit_solution(18164137805942323962)
XLA Ops:
  0.0 0.7 and_select_fusion.local_col
  0.7 0.0 copy-start
  0.7 0.1 reshape.6
  0.7 0.6 pad.4.col_message
  1.4 0.0 copy-done
  1.4 121.2 %shard_map.55 = f32[64,1664]{1,0:T(8,128)} custom-call(f32[48,128,128]{2,1,0:T(8,128)} %response.1, s32[48]{0:T(128)} %block_row.1, s32[48]{0:T(128)} %copy-done, s32[16,8,128]{2,1,0:T(8,128)} %pad.4.col_message, s32[64,1024]{1,0:T(8,128)} %counts.1, f32[13,128]{1,0:T(8,128)} %bitcast.3), custom_call_target="tpu_custom_call" | custom-call | tf_op jit(solution)/shard_map/pallas_call | solution.py:223
  122.6 1.8 %copy.9 = f32[64,1664]{1,0:T(8,128)} copy(f32[64,1664]{1,0:T(8,128)} %shard_map.55) | data formatting | bytes 851968
Async XLA Ops:
  0.7 0.7 copy-start

commit v2 on v1

v2 whole, which is shorter than its diff:
```python
import functools

import jax
import jax.numpy as jnp
from jax import lax
from jax.experimental import pallas as pl
from jax.experimental.pallas import tpu as pltpu
from jax.sharding import PartitionSpec as P

CHUNKS = 2
KINDS = 9
F32 = jnp.float32
BF16 = jnp.bfloat16
RELAY, NEAR, DENSE, AHEAD, PICK, RELAY_PICK = 0, 1, 2, 6, 7, 8


def split(x):
    high = x.astype(BF16).astype(F32)
    return jnp.concatenate([high, x - high], axis=0).astype(BF16)


def kernel(
    n, per, cols, rows, chunk_count,
    response, block_row, local_col, col_message, counts, prior,
    out,
    response_split, own_prior, priors, mass_message, mass_landed, mass_out, mass_far,
    wanted_landed, wanted, send, relay_in, near_in, dense_out, dense_in, ahead, relayed, fetched, estimate,
    ratio, inverse, send_sem, recv_sem, local_sem,
):
    blk = prior.shape[1]
    half = n // 2
    rc = counts.shape[0] // chunk_count
    me = lax.axis_index("rows")
    side = me // half
    base = side * half
    other = (1 - side) * half
    place = me - base
    partner = other + place

    def near(k):
        return lax.rem(place + k + 1, half)

    def remote(src, dst, index, peer):
        return pltpu.make_async_remote_copy(
            src_ref=src, dst_ref=dst, send_sem=send_sem.at[index], recv_sem=recv_sem.at[index],
            device_id={"rows": peer}, device_id_type=pl.DeviceIdType.MESH,
        )

    def wait_bytes(ref, sem):
        pltpu.make_async_copy(ref, ref, sem).wait()

    def sem_of(c, kind):
        return c * KINDS + kind

    PRIOR, WANTED, MASS, MASS_DENSE = (KINDS * chunk_count + i for i in range(4))
    few = pl.ds(0, (half - 1) * per)

    barrier = pltpu.get_barrier_semaphore()

    @pl.loop(0, n - 1)
    def _(k):
        pl.semaphore_signal(
            barrier, inc=1, device_id={"rows": lax.rem(me + k + 1, n)},
            device_id_type=pl.DeviceIdType.MESH,
        )

    own_prior[...] = jnp.zeros_like(own_prior)
    own_prior[0:cols, :] = prior[...]
    priors[me] = own_prior[...]

    def prepare(i, row, owner):
        for j in range(per):
            block = response[owner * per + j]
            at = row * per + j
            mass_message[i, at : at + 1, :] = jnp.sum(block, axis=0, keepdims=True)
            response_split[owner * per + j] = split(block)

    @pl.loop(0, half)
    def _(i):
        prepare(i, 0, base + i)

    pl.semaphore_wait(barrier, n - 1)

    @pl.loop(0, n - 1)
    def _(k):
        remote(own_prior, priors.at[me], PRIOR, lax.rem(me + k + 1, n)).start()

    @pl.loop(0, half)
    def _(i):
        prepare(i, 1, other + i)

    @pl.loop(0, half - 1)
    def _(k):
        q = near(k)
        remote(col_message.at[q], wanted_landed.at[place], WANTED, base + q).start()
        remote(mass_message.at[q], mass_landed.at[place], MASS, base + q).start()

    wanted_landed[place] = col_message[place]
    mass_landed[place] = mass_message[place]
    wait_bytes(priors.at[pl.ds(0, n - 1)], recv_sem.at[PRIOR])

    def fold_prior(p, total):
        for j in range(per):
            s = p * per + j
            row = priors[p, pl.ds(local_col[s], 1), :]
            spot = lax.broadcasted_iota(jnp.int32, (rows, blk), 0) == block_row[s]
            masked = jnp.where(spot, jnp.broadcast_to(row, (rows, blk)), 0.0)
            total = total + lax.dot_general(
                split(masked), response_split[s], (((1,), (1,)), ((), ())), preferred_element_type=F32
            )
        return total

    total = lax.fori_loop(0, n, fold_prior, jnp.zeros((2 * rows, 2 * blk), F32))
    total = total[:rows] + total[rows:]
    first_fold = total[:, :blk] + total[:, blk:]

    def store_ratio(c, b, folded):
        measured = counts[c * rc : (c + 1) * rc, b * blk : (b + 1) * blk].astype(F32)
        ratio[b * chunk_count + c] = split(measured / folded)

    def backward(c, phase):
        def one(s):
            x = ratio[block_row[s] * chunk_count + c]
            both = jnp.dot(
                jnp.concatenate([x, x], axis=1), response_split[s], preferred_element_type=F32
            )
            return both[:rc] + both[rc:]

        for kind, start, landing in ((RELAY, other, relay_in), (NEAR, base, near_in)):
            offset = per if kind == RELAY else 0

            @pl.loop(0, half - 1)
            def _(k):
                q = near(k)
                at = q * 2 * per + offset
                for j in range(per):
                    send[c, at + j] = one((start + q) * per + j)
                remote(
                    send.at[c, pl.ds(at, per)], landing.at[c, pl.ds(place * per, per)],
                    sem_of(c, phase * 3 + kind), base + q,
                ).start()

            for j in range(per):
                landing[c, place * per + j] = one((start + place) * per + j)

    def wait_sent(c, kinds):
        for kind in kinds:
            wait_bytes(send.at[c, few], send_sem.at[sem_of(c, kind)])

    def column_sums(landing, c, whose):
        def add(i, sums):
            sums = list(sums)
            for j in range(per):
                block = landing[c, i * per + j]
                w = wanted[i, 0, whose * per + j]
                for k in range(cols):
                    sums[k] = sums[k] + block * (w == k).astype(F32)
            return tuple(sums)

        return lax.fori_loop(0, half, add, tuple(jnp.zeros((rc, blk), F32) for _ in range(cols)))

    def relay(c, phase):
        if phase == 1:
            wait_bytes(dense_out.at[c], send_sem.at[sem_of(c, DENSE)])
        wait_bytes(relay_in.at[c, few], recv_sem.at[sem_of(c, phase * 3 + RELAY)])
        sums = column_sums(relay_in, c, 1 - side)
        for k in range(cols):
            dense_out[c, k] = sums[k]
        remote(dense_out.at[c], dense_in.at[c], sem_of(c, phase * 3 + DENSE), partner).start()

    def gather(c, phase):
        wait_bytes(near_in.at[c, few], recv_sem.at[sem_of(c, phase * 3 + NEAR)])
        sums = column_sums(near_in, c, side)
        wait_bytes(dense_in.at[c], recv_sem.at[sem_of(c, phase * 3 + DENSE)])
        return [sums[k] + dense_in[c, k] for k in range(cols)]

    def pick(c, source, whose, owner, offset, kind):
        @pl.loop(0, half - 1)
        def _(k):
            q = near(k)
            at = q * 2 * per + offset
            for j in range(per):
                send[c, at + j] = source[c, wanted[q, 0, whose * per + j]]
            remote(
                send.at[c, pl.ds(at, per)], fetched.at[c, pl.ds(owner * per, per)],
                sem_of(c, kind), base + q,
            ).start()

        for j in range(per):
            fetched[c, owner * per + j] = source[c, wanted[place, 0, whose * per + j]]

    def update(c):
        sums = gather(c, 0)
        for k in range(cols):
            estimate[c, k] = (prior[k : k + 1, :] * inverse[k : k + 1, :]) * sums[k]
        remote(estimate.at[c], ahead.at[c], sem_of(c, AHEAD), partner).start()
        wait_sent(c, (RELAY, NEAR))
        pick(c, estimate, side, me, 0, PICK)

    def relay_pick(c):
        wait_bytes(ahead.at[c], recv_sem.at[sem_of(c, AHEAD)])
        relayed[c] = ahead[c]
        pick(c, relayed, 1 - side, partner, per, RELAY_PICK)

    def fold(c):
        def add(start):
            def body(i, sums):
                sums = list(sums)
                for j in range(per):
                    s = (start + i) * per + j
                    product = lax.dot_general(
                        split(fetched[c, s]), response_split[s], (((1,), (1,)), ((), ())),
                        preferred_element_type=F32,
                    )
                    product = product[:rc] + product[rc:]
                    product = product[:, :blk] + product[:, blk:]
                    r = block_row[s]
                    for b in range(rows):
                        sums[b] = sums[b] + product * (r == b).astype(F32)
                return tuple(sums)

            return body

        sums = tuple(jnp.zeros((rc, blk), F32) for _ in range(rows))
        wait_bytes(fetched.at[c, few], recv_sem.at[sem_of(c, PICK)])
        sums = lax.fori_loop(0, half, add(base), sums)
        wait_bytes(fetched.at[c, few], recv_sem.at[sem_of(c, RELAY_PICK)])
        sums = lax.fori_loop(0, half, add(other), sums)
        for b in range(rows):
            store_ratio(c, b, sums[b])

    def masses():
        wait_bytes(wanted_landed.at[pl.ds(0, half - 1)], recv_sem.at[WANTED])
        to_scalar = pltpu.make_async_copy(wanted_landed, wanted, local_sem)
        to_scalar.start()
        to_scalar.wait()
        wait_bytes(mass_landed.at[pl.ds(0, half - 1)], recv_sem.at[MASS])

        def sums_of(row, whose):
            def add(i, sums):
                sums = list(sums)
                for j in range(per):
                    mass = mass_landed[i, row * per + j : row * per + j + 1, :]
                    w = wanted[i, 0, whose * per + j]
                    for k in range(cols):
                        sums[k] = sums[k] + mass * (w == k).astype(F32)
                return tuple(sums)

            return lax.fori_loop(0, half, add, tuple(jnp.zeros((1, blk), F32) for _ in range(cols)))

        mass_out[...] = jnp.zeros_like(mass_out)
        for k, mass in enumerate(sums_of(1, 1 - side)):
            mass_out[k : k + 1, :] = mass
        remote(mass_out, mass_far, MASS_DENSE, partner).start()
        for k, mass in enumerate(sums_of(0, side)):
            inverse[k : k + 1, :] = mass

    def efficiencies():
        wait_bytes(mass_far, recv_sem.at[MASS_DENSE])
        inverse[0:cols, :] = 1.0 / (inverse[0:cols, :] + mass_far[0:cols, :])

    def first(c):
        for b in range(rows):
            store_ratio(c, b, first_fold[b : b + 1])
        backward(c, 0)

    def second(c):
        fold(c)
        wait_sent(c, (PICK, RELAY_PICK))
        backward(c, 1)

    def finish(c):
        sums = gather(c, 1)
        for k in range(cols):
            out[c * rc : (c + 1) * rc, k * blk : (k + 1) * blk] = (
                estimate[c, k] * sums[k] * inverse[k : k + 1, :]
            )

    chunks = range(chunk_count)
    for c in chunks:
        first(c)
    masses()
    for c in chunks:
        relay(c, 0)
    efficiencies()
    for c in chunks:
        update(c)
    for c in chunks:
        relay_pick(c)
    for c in chunks:
        second(c)
    for c in chunks:
        relay(c, 1)
    for c in chunks:
        finish(c)

    for c in chunks:
        wait_sent(c, (3 + RELAY, 3 + NEAR))
        wait_bytes(dense_out.at[c], send_sem.at[sem_of(c, 3 + DENSE)])
        wait_bytes(estimate.at[c], send_sem.at[sem_of(c, AHEAD)])
    wait_bytes(priors.at[pl.ds(0, n - 1)], send_sem.at[PRIOR])
    wait_bytes(wanted_landed.at[pl.ds(0, half - 1)], send_sem.at[WANTED])
    wait_bytes(mass_landed.at[pl.ds(0, half - 1)], send_sem.at[MASS])
    wait_bytes(mass_out, send_sem.at[MASS_DENSE])


def local(response, block_row, block_col, counts, prior):
    n = lax.axis_size("rows")
    half = n // 2
    slots, blk, _ = response.shape
    per = slots // n
    reps = counts.shape[0]
    rows = counts.shape[1] // blk
    cols = prior.shape[0] // blk
    rc = reps // CHUNKS
    tall = -(-cols // 8) * 8
    mass_rows = -(-2 * per // 8) * 8
    local_col = block_col % cols
    both = local_col.reshape(2, half, per).transpose(1, 0, 2).reshape(half, 1, 2 * per)
    col_message = jnp.pad(both, ((0, 0), (0, 0), (0, blk - 2 * per)))
    vmem = pl.BlockSpec(memory_space=pltpu.VMEM)
    smem = pl.BlockSpec(memory_space=pltpu.SMEM)
    sems = KINDS * CHUNKS + 4
    return pl.pallas_call(
        functools.partial(kernel, n, per, cols, rows, CHUNKS),
        out_shape=jax.ShapeDtypeStruct((reps, cols * blk), F32),
        in_specs=[vmem, smem, smem, vmem, vmem, vmem],
        out_specs=vmem,
        scratch_shapes=[
            pltpu.VMEM((slots, 2 * blk, blk), BF16),
            pltpu.VMEM((tall, blk), F32),
            pltpu.VMEM((n, tall, blk), F32),
            pltpu.VMEM((half, mass_rows, blk), F32),
            pltpu.VMEM((half, mass_rows, blk), F32),
            pltpu.VMEM((tall, blk), F32),
            pltpu.VMEM((tall, blk), F32),
            pltpu.VMEM((half, 1, blk), jnp.int32),
            pltpu.SMEM((half, 1, blk), jnp.int32),
            pltpu.VMEM((CHUNKS, slots, rc, blk), F32),
            pltpu.VMEM((CHUNKS, half * per, rc, blk), F32),
            pltpu.VMEM((CHUNKS, half * per, rc, blk), F32),
            pltpu.VMEM((CHUNKS, cols, rc, blk), F32),
            pltpu.VMEM((CHUNKS, cols, rc, blk), F32),
            pltpu.VMEM((CHUNKS, cols, rc, blk), F32),
            pltpu.VMEM((CHUNKS, cols, rc, blk), F32),
            pltpu.VMEM((CHUNKS, slots, rc, blk), F32),
            pltpu.VMEM((CHUNKS, cols, rc, blk), F32),
            pltpu.VMEM((rows * CHUNKS, 2 * rc, blk), BF16),
            pltpu.VMEM((tall, blk), F32),
            pltpu.SemaphoreType.DMA((sems,)),
            pltpu.SemaphoreType.DMA((sems,)),
            pltpu.SemaphoreType.DMA,
        ],
        compiler_params=pltpu.CompilerParams(
            collective_id=0, has_side_effects=True, vmem_limit_bytes=60 * 1024 * 1024
        ),
    )(response, block_row, local_col, col_message, counts, prior.reshape(cols, blk))


def solution(mesh):
    in_specs = (
        P(("groups", "rows"), None, None),
        P(("groups", "rows")),
        P(("groups", "rows")),
        P(None, ("groups", "rows")),
        P(("groups", "rows")),
    )
    out_specs = P(None, ("groups", "rows"))
    return jax.shard_map(local, mesh=mesh, in_specs=in_specs, out_specs=out_specs, check_vma=False)
```

time: 125 us -> 105 us (0.84)
  the two profiles are of different devices: /device:TPU:21 before, /device:TPU:1 now
where the time goes in v2:
time: 105 us; the launch traced here: 104 us
  Pallas kernels  101 us (96%)
  local copies, waits for them, and re-layouts  2.57 us (2%)
    pallas_call x1, Pallas kernels, local(): pl.pallas_call(functools.partial(kernel, n, per, cols, rows, CHUNKS), out...  101 us

profile of v2, /device:TPU:1, one launch (start us, length us, event | category | flops | bytes accessed | tf_op | source)
XLA Modules:
  0.0 104.4 jit_solution(779962554183396356)
XLA Ops:
  0.0 0.7 and_select_fusion.local_col
  0.7 0.0 copy-start
  0.7 0.1 reshape.9
  0.8 0.1 reshape.12
  0.9 0.6 pad.4.col_message
  1.5 0.0 copy-done
  1.5 101.1 %shard_map.55 = f32[64,1664]{1,0:T(8,128)} custom-call(f32[48,128,128]{2,1,0:T(8,128)} %response.1, s32[48]{0:T(128)} %block_row.1, s32[48]{0:T(128)} %copy-done, s32[8,1,128]{2,1,0:T(1,128)} %pad.4.col_message, s32[64,1024]{1,0:T(8,128)} %counts.1, f32[13,128]{1,0:T(8,128)} %bitcast.3), custom_call_target="tpu_custom_call" | custom-call | tf_op jit(solution)/shard_map/pallas_call | solution.py:324
  102.6 1.8 %copy.13 = f32[64,1664]{1,0:T(8,128)} copy(f32[64,1664]{1,0:T(8,128)} %shard_map.55) | data formatting | bytes 851968
  (1 shorter events, 0.0 us)
Async XLA Ops:
  0.7 0.8 copy-start

commit v3 on v2

--- a/solution.py
+++ b/solution.py
@@ -21,11 +21,11 @@
 
 def kernel(
     n, per, cols, rows, chunk_count,
-    response, block_row, local_col, col_message, counts, prior,
+    response_hbm, block_row, block_col, counts, prior,
     out,
-    response_split, own_prior, priors, mass_message, mass_landed, mass_out, mass_far,
+    response, response_split, col_message, own_prior, priors, mass_message, mass_landed, mass_out, mass_far,
     wanted_landed, wanted, send, relay_in, near_in, dense_out, dense_in, ahead, relayed, fetched, estimate,
-    ratio, inverse, send_sem, recv_sem, local_sem,
+    ratio, inverse, send_sem, recv_sem, local_sem, load_sem,
 ):
     blk = prior.shape[1]
     half = n // 2
@@ -40,6 +40,13 @@
     def near(k):
         return lax.rem(place + k + 1, half)
 
+    def load(start, i):
+        part = pl.ds(start * per, half * per)
+        return pltpu.make_async_copy(response_hbm.at[part], response.at[part], load_sem.at[i])
+
+    load(base, 0).start()
+    load(other, 1).start()
+
     def remote(src, dst, index, peer):
         return pltpu.make_async_remote_copy(
             src_ref=src, dst_ref=dst, send_sem=send_sem.at[index], recv_sem=recv_sem.at[index],
@@ -75,15 +82,31 @@
             mass_message[i, at : at + 1, :] = jnp.sum(block, axis=0, keepdims=True)
             response_split[owner * per + j] = split(block)
 
+    pl.semaphore_wait(barrier, n - 1)
+
+    @pl.loop(0, n - 1)
+    def _(k):
+        remote(own_prior, priors.at[me], PRIOR, lax.rem(me + k + 1, n)).start()
+
+    lane = lax.broadcasted_iota(jnp.int32, (1, blk), 1)
+
+    @pl.loop(0, half)
+    def _(i):
+        line = jnp.zeros((1, blk), jnp.int32)
+        for t in range(2):
+            for j in range(per):
+                owner = t * half + i
+                value = lax.rem(block_col[owner * per + j], cols)
+                line = jnp.where(lane == t * per + j, value, line)
+        col_message[i] = line
+
+    load(base, 0).wait()
+
     @pl.loop(0, half)
     def _(i):
         prepare(i, 0, base + i)
 
-    pl.semaphore_wait(barrier, n - 1)
-
-    @pl.loop(0, n - 1)
-    def _(k):
-        remote(own_prior, priors.at[me], PRIOR, lax.rem(me + k + 1, n)).start()
+    load(other, 1).wait()
 
     @pl.loop(0, half)
     def _(i):
@@ -102,7 +125,7 @@
     def fold_prior(p, total):
         for j in range(per):
             s = p * per + j
-            row = priors[p, pl.ds(local_col[s], 1), :]
+            row = priors[p, pl.ds(lax.rem(block_col[s], cols), 1), :]
             spot = lax.broadcasted_iota(jnp.int32, (rows, blk), 0) == block_row[s]
             masked = jnp.where(spot, jnp.broadcast_to(row, (rows, blk)), 0.0)
             total = total + lax.dot_general(
@@ -110,7 +133,7 @@
             )
         return total
 
-    total = lax.fori_loop(0, n, fold_prior, jnp.zeros((2 * rows, 2 * blk), F32))
+    total = lax.fori_loop(0, n, fold_prior, jnp.zeros((2 * rows, 2 * blk), F32), unroll=4)
     total = total[:rows] + total[rows:]
     first_fold = total[:, :blk] + total[:, blk:]
 
@@ -118,7 +141,7 @@
         measured = counts[c * rc : (c + 1) * rc, b * blk : (b + 1) * blk].astype(F32)
         ratio[b * chunk_count + c] = split(measured / folded)
 
-    def backward(c, phase):
+    def backward(c, phase, kinds=((RELAY, other, relay_in), (NEAR, base, near_in))):
         def one(s):
             x = ratio[block_row[s] * chunk_count + c]
             both = jnp.dot(
@@ -126,10 +149,10 @@
             )
             return both[:rc] + both[rc:]
 
-        for kind, start, landing in ((RELAY, other, relay_in), (NEAR, base, near_in)):
+        for kind, start, landing in kinds:
             offset = per if kind == RELAY else 0
 
-            @pl.loop(0, half - 1)
+            @pl.loop(0, half - 1, unroll=7)
             def _(k):
                 q = near(k)
                 at = q * 2 * per + offset
@@ -223,9 +246,9 @@
 
         sums = tuple(jnp.zeros((rc, blk), F32) for _ in range(rows))
         wait_bytes(fetched.at[c, few], recv_sem.at[sem_of(c, PICK)])
-        sums = lax.fori_loop(0, half, add(base), sums)
+        sums = lax.fori_loop(0, half, add(base), sums, unroll=4)
         wait_bytes(fetched.at[c, few], recv_sem.at[sem_of(c, RELAY_PICK)])
-        sums = lax.fori_loop(0, half, add(other), sums)
+        sums = lax.fori_loop(0, half, add(other), sums, unroll=4)
         for b in range(rows):
             store_ratio(c, b, sums[b])
 
@@ -278,7 +301,11 @@
 
     chunks = range(chunk_count)
     for c in chunks:
-        first(c)
+        for b in range(rows):
+            store_ratio(c, b, first_fold[b : b + 1])
+        backward(c, 0, ((RELAY, other, relay_in),))
+    for c in chunks:
+        backward(c, 0, ((NEAR, base, near_in),))
     masses()
     for c in chunks:
         relay(c, 0)
@@ -289,7 +316,6 @@
         relay_pick(c)
     for c in chunks:
         second(c)
-    for c in chunks:
         relay(c, 1)
     for c in chunks:
         finish(c)
@@ -315,19 +341,18 @@
     rc = reps // CHUNKS
     tall = -(-cols // 8) * 8
     mass_rows = -(-2 * per // 8) * 8
-    local_col = block_col % cols
-    both = local_col.reshape(2, half, per).transpose(1, 0, 2).reshape(half, 1, 2 * per)
-    col_message = jnp.pad(both, ((0, 0), (0, 0), (0, blk - 2 * per)))
     vmem = pl.BlockSpec(memory_space=pltpu.VMEM)
     smem = pl.BlockSpec(memory_space=pltpu.SMEM)
     sems = KINDS * CHUNKS + 4
     return pl.pallas_call(
         functools.partial(kernel, n, per, cols, rows, CHUNKS),
         out_shape=jax.ShapeDtypeStruct((reps, cols * blk), F32),
-        in_specs=[vmem, smem, smem, vmem, vmem, vmem],
+        in_specs=[pl.BlockSpec(memory_space=pl.ANY), smem, smem, vmem, vmem],
         out_specs=vmem,
         scratch_shapes=[
+            pltpu.VMEM((slots, blk, blk), F32),
             pltpu.VMEM((slots, 2 * blk, blk), BF16),
+            pltpu.VMEM((half, 1, blk), jnp.int32),
             pltpu.VMEM((tall, blk), F32),
             pltpu.VMEM((n, tall, blk), F32),
             pltpu.VMEM((half, mass_rows, blk), F32),
@@ -350,11 +375,12 @@
             pltpu.SemaphoreType.DMA((sems,)),
             pltpu.SemaphoreType.DMA((sems,)),
             pltpu.SemaphoreType.DMA,
+            pltpu.SemaphoreType.DMA((2,)),
         ],
         compiler_params=pltpu.CompilerParams(
             collective_id=0, has_side_effects=True, vmem_limit_bytes=60 * 1024 * 1024
         ),
-    )(response, block_row, local_col, col_message, counts, prior.reshape(cols, blk))
+    )(response, block_row, block_col, counts, prior.reshape(cols, blk))
 
 
 def solution(mesh):

time: 105 us -> 99.4 us (0.947)
  Pallas kernels: 101 us -> 97 us
    pallas_call x1, Pallas kernels: 101 us -> 97 us  [local(): pl.pallas_call(functools.partial(kernel, n, per, cols, rows, CHUNKS), out...]
where the time goes in v3:
time: 99.4 us; the launch traced here: 98.8 us
  Pallas kernels  97 us (98%)
  local copies, waits for them, and re-layouts  1.79 us (2%)
    pallas_call x1, Pallas kernels, local(): pl.pallas_call(functools.partial(kernel, n, per, cols, rows, CHUNKS), out...  97 us

profile of v3, /device:TPU:1, one launch (start us, length us, event | category | flops | bytes accessed | tf_op | source)
XLA Modules:
  0.0 98.8 jit_solution(2941587289787828785)
XLA Ops:
  0.0 97.0 %shard_map.55 = f32[64,1664]{1,0:T(8,128)} custom-call(f32[48,128,128]{2,1,0:T(8,128)} %response_hbm.1, s32[48]{0:T(128)} %block_row.1, s32[48]{0:T(128)} %block_col.1, s32[64,1024]{1,0:T(8,128)} %counts.1, f32[13,128]{1,0:T(8,128)} %bitcast.1), custom_call_target="tpu_custom_call" | custom-call | tf_op jit(solution)/shard_map/pallas_call | solution.py:347
  97.0 1.8 %copy.7 = f32[64,1664]{1,0:T(8,128)} copy(f32[64,1664]{1,0:T(8,128)} %shard_map.55) | data formatting | bytes 851968

commit v4 on v3

--- a/solution.py
+++ b/solution.py
@@ -282,16 +282,6 @@
         wait_bytes(mass_far, recv_sem.at[MASS_DENSE])
         inverse[0:cols, :] = 1.0 / (inverse[0:cols, :] + mass_far[0:cols, :])
 
-    def first(c):
-        for b in range(rows):
-            store_ratio(c, b, first_fold[b : b + 1])
-        backward(c, 0)
-
-    def second(c):
-        fold(c)
-        wait_sent(c, (PICK, RELAY_PICK))
-        backward(c, 1)
-
     def finish(c):
         sums = gather(c, 1)
         for k in range(cols):
@@ -315,8 +305,12 @@
     for c in chunks:
         relay_pick(c)
     for c in chunks:
-        second(c)
+        fold(c)
+        wait_sent(c, (PICK, RELAY_PICK))
+        backward(c, 1, ((RELAY, other, relay_in),))
+    for c in chunks:
         relay(c, 1)
+        backward(c, 1, ((NEAR, base, near_in),))
     for c in chunks:
         finish(c)
 

time: 99.4 us -> 95.6 us (0.962)
  Pallas kernels: 97 us -> 93.7 us
    pallas_call x1, Pallas kernels: 97 us -> 93.7 us  [local(): pl.pallas_call(functools.partial(kernel, n, per, cols, rows, CHUNKS), out...]
where the time goes in v4:
time: 95.6 us; the launch traced here: 95.5 us
  Pallas kernels  93.7 us (98%)
  local copies, waits for them, and re-layouts  1.79 us (2%)
    pallas_call x1, Pallas kernels, local(): pl.pallas_call(functools.partial(kernel, n, per, cols, rows, CHUNKS), out...  93.7 us

profile of v4, /device:TPU:1, one launch (start us, length us, event | category | flops | bytes accessed | tf_op | source)
XLA Modules:
  0.0 95.5 jit_solution(268815531188274327)
XLA Ops:
  0.0 93.7 %shard_map.55 = f32[64,1664]{1,0:T(8,128)} custom-call(f32[48,128,128]{2,1,0:T(8,128)} %response_hbm.1, s32[48]{0:T(128)} %block_row.1, s32[48]{0:T(128)} %block_col.1, s32[64,1024]{1,0:T(8,128)} %counts.1, f32[13,128]{1,0:T(8,128)} %bitcast.1), custom_call_target="tpu_custom_call" | custom-call | tf_op jit(solution)/shard_map/pallas_call | solution.py:341
  93.7 1.8 %copy.7 = f32[64,1664]{1,0:T(8,128)} copy(f32[64,1664]{1,0:T(8,128)} %shard_map.55) | data formatting | bytes 851968

commit v5 on v4

--- a/solution.py
+++ b/solution.py
@@ -21,9 +21,9 @@
 
 def kernel(
     n, per, cols, rows, chunk_count,
-    response_hbm, block_row, block_col, counts, prior,
+    response_hbm, block_row, block_col, counts_hbm, prior,
     out,
-    response, response_split, col_message, own_prior, priors, mass_message, mass_landed, mass_out, mass_far,
+    counts, response, response_split, col_message, own_prior, priors, mass_message, mass_landed, mass_out, mass_far,
     wanted_landed, wanted, send, relay_in, near_in, dense_out, dense_in, ahead, relayed, fetched, estimate,
     ratio, inverse, send_sem, recv_sem, local_sem, load_sem,
 ):
@@ -46,6 +46,8 @@
 
     load(base, 0).start()
     load(other, 1).start()
+    load_counts = pltpu.make_async_copy(counts_hbm, counts, load_sem.at[2])
+    load_counts.start()
 
     def remote(src, dst, index, peer):
         return pltpu.make_async_remote_copy(
@@ -136,6 +138,7 @@
     total = lax.fori_loop(0, n, fold_prior, jnp.zeros((2 * rows, 2 * blk), F32), unroll=4)
     total = total[:rows] + total[rows:]
     first_fold = total[:, :blk] + total[:, blk:]
+    load_counts.wait()
 
     def store_ratio(c, b, folded):
         measured = counts[c * rc : (c + 1) * rc, b * blk : (b + 1) * blk].astype(F32)
@@ -336,14 +339,16 @@
     tall = -(-cols // 8) * 8
     mass_rows = -(-2 * per // 8) * 8
     vmem = pl.BlockSpec(memory_space=pltpu.VMEM)
+    hbm = pl.BlockSpec(memory_space=pl.ANY)
     smem = pl.BlockSpec(memory_space=pltpu.SMEM)
     sems = KINDS * CHUNKS + 4
     return pl.pallas_call(
         functools.partial(kernel, n, per, cols, rows, CHUNKS),
         out_shape=jax.ShapeDtypeStruct((reps, cols * blk), F32),
-        in_specs=[pl.BlockSpec(memory_space=pl.ANY), smem, smem, vmem, vmem],
+        in_specs=[hbm, smem, smem, hbm, vmem],
         out_specs=vmem,
         scratch_shapes=[
+            pltpu.VMEM(counts.shape, counts.dtype),
             pltpu.VMEM((slots, blk, blk), F32),
             pltpu.VMEM((slots, 2 * blk, blk), BF16),
             pltpu.VMEM((half, 1, blk), jnp.int32),
@@ -369,7 +374,7 @@
             pltpu.SemaphoreType.DMA((sems,)),
             pltpu.SemaphoreType.DMA((sems,)),
             pltpu.SemaphoreType.DMA,
-            pltpu.SemaphoreType.DMA((2,)),
+            pltpu.SemaphoreType.DMA((3,)),
         ],
         compiler_params=pltpu.CompilerParams(
             collective_id=0, has_side_effects=True, vmem_limit_bytes=60 * 1024 * 1024

time: 95.6 us -> 95.4 us (level)
  no operation moved by 1% of the time
where the time goes in v5:
time: 95.4 us; the launch traced here: 95.2 us
  Pallas kernels  93.4 us (98%)
  local copies, waits for them, and re-layouts  1.79 us (2%)
    pallas_call x1, Pallas kernels, local(): pl.pallas_call(functools.partial(kernel, n, per, cols, rows, CHUNKS), out...  93.4 us

profile of v5, /device:TPU:1, one launch (start us, length us, event | category | flops | bytes accessed | tf_op | source)
XLA Modules:
  0.0 95.2 jit_solution(2565791944578657172)
XLA Ops:
  0.0 93.4 %shard_map.55 = f32[64,1664]{1,0:T(8,128)} custom-call(f32[48,128,128]{2,1,0:T(8,128)} %response_hbm.1, s32[48]{0:T(128)} %block_row.1, s32[48]{0:T(128)} %block_col.1, s32[64,1024]{1,0:T(8,128)} %counts_hbm.1, f32[13,128]{1,0:T(8,128)} %bitcast.1), custom_call_target="tpu_custom_call" | custom-call | tf_op jit(solution)/shard_map/pallas_call | solution.py:345
  93.4 1.8 %copy.7 = f32[64,1664]{1,0:T(8,128)} copy(f32[64,1664]{1,0:T(8,128)} %shard_map.55) | data formatting | bytes 851968
